TPU v7x, 32 devices: a whole 2x2x4 slice. The times are simulated.
32 devices in a mesh: groups: 2 (over y), dev: 8 (over z, x), tp: 1, sub: 2 (over core).
Axes of the slice: x: 2, y: 2, z: 4, core: 2. Of those that a mesh axis runs over, the one named last changes fastest.
Arguments:
- hidden: bfloat16 [256, 4096], P(('groups', 'dev'), ('tp', 'sub')), parts along dimension 0, may hold values from -8 to 8
- new_query: bfloat16 [256, 4096], P(('groups', 'tp', 'sub'), 'dev'), parts along dimension 0, may hold values from -6 to 6
- new_key: bfloat16 [256, 4096], P(('groups', 'tp', 'sub'), 'dev'), parts along dimension 0, may hold values from -6 to 6
- new_value: bfloat16 [256, 4096], P(('groups', 'tp', 'sub'), 'dev'), parts along dimension 0, may hold values from -6 to 6
- out_gate: bfloat16 [256, 4096], P(('groups', 'tp', 'sub'), 'dev'), parts along dimension 0, may hold values from -6 to 6
- states: bfloat16 [256, 32, 128, 128], P(('groups', 'tp', 'sub'), 'dev'), parts along dimension 0, may hold values from -6 to 6
- decay_rate: float32 [32], P('dev'), may hold values from 0.03 to 3
- out_proj: bfloat16 [4096, 4096], P('dev', ('tp', 'sub')), may hold values from -0.09375 to 0.09375
- norm_gain: float32 [4096], P(('tp', 'sub')), may hold values from 0.5 to 2
- routes: int32 [256, 2], P(('groups', 'dev')), parts along dimension 0, may hold values from 0 to 3, all different within a row; in each aligned block of 16 rows (0 to 15, 16 to 31, ...) at most 16 rows name the same one
- route_weight: float32 [256, 2], P(('groups', 'dev')), parts along dimension 0, may hold values from 0.2 to 1
- expert_gate: bfloat16 [8, 4096, 2304], P('dev', ('tp', 'sub')), may hold values from -0.09375 to 0.09375
- expert_up: bfloat16 [8, 4096, 2304], P('dev', ('tp', 'sub')), may hold values from -0.09375 to 0.09375
- expert_down: bfloat16 [8, 2304, 4096], P('dev', None, ('tp', 'sub')), may hold values from -0.09375 to 0.09375
Outputs:
- mixed: bfloat16 [256, 4096], P(('groups', 'dev'), ('tp', 'sub')), parts along dimension 0
- new_states: bfloat16 [256, 32, 128, 128], P(('groups', 'tp', 'sub'), 'dev'), parts along dimension 0
There are 2 independent parts, one for each index of `groups`. A program takes and returns all parts, laid end to end along the dimension named above; an argument that names none is the same for every part. Nothing has to cross between parts.
Inputs may be any that keep to these rules, and one draw needn't show every extreme that they name: `routes`: the 2 experts of a request differ. In the rows of one index of dev (16 requests) no expert is named by more than 16 rows, a bound that some block reaches.
All inputs are finite; a program needn't handle non-finite values.
Results may differ from a plain program's by a relative error of at most 0.012.
Values may be sent and summed in bfloat16 or wider, within the bound.
A program may use at most 128 MiB of HBM per device.

v0:
```python
import jax
import jax.numpy as jnp
from jax import lax
from jax.sharding import PartitionSpec as P

D = 4096
SPLIT = 2


EPS = 1e-06


def route_tables(routes, route_weight, experts, slots):
    expert_ids = jnp.arange(experts, dtype=jnp.int32)
    chosen = routes[:, :, None] == expert_ids[None, None, :]
    member = jnp.any(chosen, axis=1).astype(jnp.int32)
    position = jnp.cumsum(member, axis=0) - member
    slot_ids = jnp.arange(slots, dtype=jnp.int32)
    placed = (member[:, :, None] == 1) & (position[:, :, None] == slot_ids[None, None, :])
    weights = jnp.sum(jnp.where(chosen, route_weight[:, :, None], jnp.float32(0.0)), axis=1)
    return (placed, weights)


def shards(
    hidden,
    new_query,
    new_key,
    new_value,
    out_gate,
    states,
    decay_rate,
    out_proj,
    norm_gain,
    routes,
    route_weight,
    expert_gate,
    expert_up,
    expert_down,
):
    local_reqs = states.shape[0]
    heads_here = states.shape[1]
    head_size = states.shape[3]
    query_heads = new_query.astype(jnp.float32).reshape(
        local_reqs, heads_here, head_size
    ) * head_size ** (-0.5)
    key_heads = new_key.astype(jnp.float32).reshape(local_reqs, heads_here, head_size)
    value_heads = new_value.astype(jnp.float32).reshape(local_reqs, heads_here, head_size)
    retain = jnp.exp(-decay_rate)
    updated = (
        retain[None, :, None, None] * states.astype(jnp.float32)
        + key_heads[:, :, :, None] * value_heads[:, :, None, :]
    )
    readout = jnp.einsum("rhi,rhij->rhj", query_heads, updated, precision=lax.Precision.HIGHEST)
    head_out = (
        jax.nn.sigmoid(out_gate.astype(jnp.float32))
        * readout.reshape(local_reqs, heads_here * head_size)
    ).astype(jnp.bfloat16)
    new_states = updated.astype(jnp.bfloat16)
    all_heads = lax.all_gather(head_out, ("tp", "sub"), axis=0, tiled=True)
    rows_here = hidden.shape[0]
    attended = lax.psum_scatter(
        jnp.dot(all_heads, out_proj, preferred_element_type=jnp.float32),
        "dev",
        scatter_dimension=0,
        tiled=True,
    )
    residual = (hidden.astype(jnp.float32) + attended).astype(jnp.bfloat16)
    feature_count = residual.shape[1]
    experts = lax.axis_size("dev") // SPLIT
    top_count = routes.shape[1]
    slots = min(rows_here, 2 * ((rows_here * top_count + experts - 1) // experts))
    placed, weights = route_tables(routes, route_weight, experts, slots)
    picks = placed.astype(jnp.bfloat16)
    outgoing = jnp.einsum(
        "nec,nd->ecd", picks, residual, preferred_element_type=jnp.float32
    ).astype(jnp.bfloat16)
    outgoing = jnp.repeat(outgoing, SPLIT, axis=0)
    received = lax.all_to_all(outgoing, "dev", split_axis=0, concat_axis=0, tiled=True)
    sources, count, width = received.shape
    flat_rows = received.reshape(sources * count, width).astype(jnp.float32)
    scaled = (flat_rows * norm_gain[None, :]).astype(jnp.bfloat16)
    gate_part = jnp.dot(scaled, expert_gate[0], preferred_element_type=jnp.float32)
    up_part = jnp.dot(scaled, expert_up[0], preferred_element_type=jnp.float32)
    squares = jnp.sum(flat_rows * flat_rows, axis=1)
    gate_sum, up_sum, square_sum = lax.psum((gate_part, up_part, squares), ("tp", "sub"))
    inverse = lax.rsqrt(square_sum / D + EPS)[:, None]
    act = (jax.nn.silu(inverse * gate_sum) * (inverse * up_sum)).astype(jnp.bfloat16)
    produced = jnp.dot(act, expert_down[0], preferred_element_type=jnp.float32)
    expert_out = produced.reshape(sources, count, width)
    returned = lax.all_to_all(expert_out, "dev", split_axis=0, concat_axis=0, tiled=True)
    merged = returned.reshape(experts, SPLIT, slots, feature_count).sum(axis=1)
    coeff = placed.astype(jnp.float32) * weights[:, :, None]
    mixture = jnp.einsum("nec,ecd->nd", coeff, merged, precision=lax.Precision.HIGHEST)
    mixed = (residual.astype(jnp.float32) + mixture).astype(jnp.bfloat16)
    return (mixed, new_states)


def solution(mesh):
    placed = (
        P(("groups", "dev"), ("tp", "sub")),
        P(("groups", "tp", "sub"), "dev"),
        P(("groups", "tp", "sub"), "dev"),
        P(("groups", "tp", "sub"), "dev"),
        P(("groups", "tp", "sub"), "dev"),
        P(("groups", "tp", "sub"), "dev", None, None),
        P("dev"),
        P("dev", ("tp", "sub")),
        P(("tp", "sub")),
        P(("groups", "dev"), None),
        P(("groups", "dev"), None),
        P("dev", ("tp", "sub"), None),
        P("dev", ("tp", "sub"), None),
        P("dev", None, ("tp", "sub")),
    )
    return jax.shard_map(
        shards,
        mesh=mesh,
        in_specs=placed,
        out_specs=(
            P(("groups", "dev"), ("tp", "sub")),
            P(("groups", "tp", "sub"), "dev", None, None),
        ),
        check_vma=False,
    )
```

profile of v0, /device:TPU:0, one launch (start us, length us, event | category | flops | bytes accessed | tf_op | source)
XLA Modules:
  0.0 195.2 jit_solution(1574253932069123664)
XLA Ops:
  7.2 0.8 negate_exponential_fusion
  8.0 0.9 reshape.58
  8.9 0.9 reshape.59
  9.8 0.9 convert_multiply_fusion.2
  10.8 17.8 %fusion.1 = f32[64,4,1,128]{3,2,1,0:T(1,128)S(1)} fusion(f32[64,4,128,1]{2,3,1,0:T(1,128)S(1)} %bitcast.45, bf16[64,4,128,128]{3,2,1,0:T(8,128)(2,1)} %param.19, f32[64,4,128]{2,1,0:T(4,128)S(1)} %reshape.59, f32[64,4,128]{2,1,0:T(4,128)S(1)} %reshape.58, f32[4]{0:T(128)S(1)} %negate_exponential_fusion), kind=kOutput, calls=%fused_computation.2 | convolution fusion | flops 67108864 | bytes 8912912 | tf_op jit(solution)/shard_map/rhi,rhij->rhj/dot_general | solution.py:53
  28.6 2.0 %all_gather.3 = bf16[128,512]{1,0:T(8,128)(2,1)S(1)} all-gather(bf16[64,512]{1,0:T(8,128)(2,1)S(1)} %fusion.15), channel_id=1, replica_groups=mesh['groups'=2,'dev'=8,'tp'=1,'sub'=2] {'tp','sub'}, dimensions={0}, use_global_device_ids=true | all-gather | bytes 196608 | tf_op jit(solution)/shard_map/all_gather | solution.py:59
  30.6 1.4 fusion.29
  32.1 0.1 copy.21
  32.2 0.1 copy.22
  32.4 0.1 copy.23
  32.5 65.9 %reduce-scatter.2.cloned.1.call-done = f32[16,2048]{1,0:T(8,128)} async-done(((f32[128,2048]{1,0:T(8,128)}), f32[16,2048]{1,0:T(8,128)}) %reduce-scatter.2.cloned.1.call-update) | async-done | bytes 131088 | tf_op jit(solution)/shard_map/reduce_scatter | solution.py:61
  98.3 1.2 convolution_convert_fusion
  99.6 16.3 %all_to_all.10 = bf16[8,16,2048]{2,1,0:T(8,128)(2,1)S(1)} all-to-all(bf16[8,16,2048]{2,1,0:T(8,128)(2,1)S(1)} %bitcast.44), channel_id=1, replica_groups=mesh['groups'=2,'dev'=8,'tp'=1,'sub'=2] {'dev'}, dimensions={0} | all-to-all | bytes 1048576 | tf_op jit(solution)/shard_map/all_to_all | solution.py:78
  115.9 0.2 fusion.13
  116.2 6.3 %fusion.4 = f32[128,2304]{1,0:T(8,128)} fusion(bf16[128,2048]{1,0:T(8,128)(2,1)S(1)} %bitcast.41, bf16[1,2048,2304]{2,1,0:T(8,128)(2,1)} %param.26), kind=kOutput, calls=%fused_computation.5 | convolution fusion | flops 1207959552 | bytes 11141120 | tf_op jit(solution)/shard_map/dot_general | solution.py:83
  122.5 2.5 %fusion.6 = f32[128,2304]{1,0:T(8,128)} fusion(bf16[128,2048]{1,0:T(8,128)(2,1)S(1)} %bitcast.42, bf16[1,2048,2304]{2,1,0:T(8,128)(2,1)S(1)} %bitcast.40), kind=kOutput, calls=%fused_computation.7 | convolution fusion | flops 1207959552 | bytes 11141120 | tf_op jit(solution)/shard_map/dot_general | solution.py:82
  125.0 2.6 %psum.21 = f32[128]{0:T(128)S(1)} all-reduce(f32[128]{0:T(128)S(1)} %reduce_sum.31), channel_id=1, replica_groups=mesh['groups'=2,'dev'=8,'tp'=1,'sub'=2] {'tp','sub'}, use_global_device_ids=true, to_apply=%region_5.6 | all-reduce | flops 128 | bytes 1024 | tf_op jit(solution)/shard_map/psum | solution.py:85
  127.6 18.2 %all-reduce.3.cloned.1.call-done = (f32[128,2304]{1,0:T(8,128)}, f32[128,2304]{1,0:T(8,128)}) async-done(((f32[128,2304]{1,0:T(8,128)}, f32[128,2304]{1,0:T(8,128)}), (f32[128,2304]{1,0:T(8,128)}, f32[128,2304]{1,0:T(8,128)})) %all-reduce.3.cloned.1.call-update) | async-done | bytes 2359312 | tf_op jit(solution)/shard_map/psum | solution.py:85
  145.8 2.0 %multiply_convert_fusion = bf16[128,2304]{1,0:T(8,128)(2,1)S(1)} fusion(f32[128,2304]{1,0:T(8,128)} %get-tuple-element.2, f32[128,2304]{1,0:T(8,128)} %get-tuple-element.3, f32[128]{0:T(128)S(1)} %add_rsqrt_fusion), kind=kLoop, calls=%fused_computation.18 | loop fusion | flops 2359296 | bytes 2949632 | tf_op jit(solution)/shard_map/convert_element_type | solution.py:87
  147.9 6.2 %fusion.2 = f32[8,16,2048]{2,1,0:T(8,128)} fusion(bf16[8,16,2304]{2,1,0:T(8,128)(2,1)S(1)} %bitcast.43, bf16[1,2304,2048]{2,1,0:T(8,128)(2,1)} %param.27), kind=kOutput, calls=%fused_computation.3 | convolution fusion | flops 1207959552 | bytes 11075584 | tf_op jit(solution)/shard_map/dot_general | solution.py:88
  154.0 5.8 %all-to-all-start.1 = ((f32[8,16,2048]{2,1,0:T(8,128)}), f32[8,16,2048]{2,1,0:T(8,128)S(1)}, u32[]{:S(2)}, u32[]{:S(2)}) async-start(f32[8,16,2048]{2,1,0:T(8,128)} %fusion.2), calls=%async_computation.2 | async-start | bytes 2097152 | tf_op jit(solution)/shard_map/all_to_all | solution.py:90
  159.8 8.6 %fusion = bf16[64,4,128,128]{3,2,1,0:T(8,128)(2,1)} fusion(bf16[64,4,128,128]{3,2,1,0:T(8,128)(2,1)} %param.19, f32[64,4,128]{2,1,0:T(4,128)S(1)} %reshape.59, f32[64,4,128]{2,1,0:T(4,128)S(1)} %reshape.58, f32[4]{0:T(128)S(1)} %negate_exponential_fusion), kind=kLoop, calls=%fused_computation.1 | loop fusion | flops 20971520 | bytes 17039376 | tf_op jit(solution)/shard_map/convert_element_type | solution.py:58
  168.4 17.6 %all-to-all-done.1 = f32[8,16,2048]{2,1,0:T(8,128)S(1)} async-done(((f32[8,16,2048]{2,1,0:T(8,128)}), f32[8,16,2048]{2,1,0:T(8,128)S(1)}, u32[]{:S(2)}, u32[]{:S(2)}) %all-to-all-start.1) | async-done | bytes 1048608 | tf_op jit(solution)/shard_map/all_to_all | solution.py:90
  186.1 2.2 %fusion.12 = bf16[16,2048]{1,0:T(8,128)(2,1)} fusion(f32[4,16,2048]{2,1,0:T(8,128)S(1)} %bitcast_reduce_fusion, f32[16,4]{0,1:T(4,128)S(1)} %select_reduce_fusion, s32[16,4]{0,1:T(4,128)S(1)} %copy.23, pred[16,4]{0,1:T(4,128)(4,1)S(1)} %copy.22, f32[16,2048]{1,0:T(8,128)S(1)} %copy-done.1, bf16[16,2048]{1,0:T(8,128)(2,1)} %param.14), kind=kOutput, calls=%fused_computation.15 | convolution fusion | flops 25365504 | bytes 787008 | tf_op jit(solution)/shard_map/nec,ecd->nd/dot_general | solution.py:93
  (36 shorter events, 0.5 us)
Async XLA Ops:
  7.2 23.4 %copy-start = (bf16[512,2048]{1,0:T(8,128)(2,1)S(1)}, bf16[512,2048]{1,0:T(8,128)(2,1)}, u32[]{:S(2)}) copy-start(bf16[512,2048]{1,0:T(8,128)(2,1)} %param.21) | copy-start | bytes 6291460
  7.2 91.2 %reduce-scatter.2.cloned.1.call-start = ((), (), s32[]{:S(2)}) async-start(), calls=%async_computation.3 | async-start | bytes 1179648 | tf_op jit(solution)/shard_map/reduce_scatter | solution.py:61
  10.7 17.8 %copy-start.3 = (bf16[64,512]{1,0:T(8,128)(2,1)S(1)}, bf16[64,512]{1,0:T(8,128)(2,1)}, u32[]{:S(2)}) copy-start(bf16[64,512]{1,0:T(8,128)(2,1)} %param.18) | copy-start | bytes 196612
  10.7 21.4 %copy-start.5 = (s32[16,2]{0,1:T(2,128)S(1)}, s32[16,2]{0,1:T(2,128)}, u32[]{:S(2)}) copy-start(s32[16,2]{0,1:T(2,128)} %param.23) | copy-start | bytes 388
  10.7 87.6 %copy-start.2 = (bf16[16,2048]{1,0:T(8,128)(2,1)S(1)}, bf16[16,2048]{1,0:T(8,128)(2,1)}, u32[]{:S(2)}) copy-start(bf16[16,2048]{1,0:T(8,128)(2,1)} %param.14) | copy-start | bytes 196612
  10.7 105.2 %copy-start.4 = (f32[2048]{0:T(1024)S(1)}, f32[2048]{0:T(1024)}, u32[]{:S(2)}) copy-start(f32[2048]{0:T(1024)} %param.22) | copy-start | bytes 24580
  32.0 113.8 %all-reduce.3.cloned.1.call-start = ((), (), s32[]{:S(2)}) async-start(), calls=%async_computation.4 | async-start | bytes 4718592 | tf_op jit(solution)/shard_map/psum | solution.py:85
  115.9 6.5 %slice-start = ((s8[9437184]{0:T(1024)(128)(4,1)}), s8[4194304]{0:T(1024)(128)(4,1)S(1)}, s32[]{:S(2)}) async-start(s8[9437184]{0:T(1024)(128)(4,1)} %bitcast.39), calls=%async_computation.5 | async-start | bytes 8388608
  116.2 6.3 %slice-start.1 = ((s8[9437184]{0:T(1024)(128)(4,1)}), s8[4194304]{0:T(1024)(128)(4,1)S(1)}, s32[]{:S(2)}) async-start(s8[9437184]{0:T(1024)(128)(4,1)} %bitcast.39), calls=%async_computation.6 | async-start | bytes 8388608
  116.2 6.3 %slice-start.2 = ((s8[9437184]{0:T(1024)(128)(4,1)}), s8[1048576]{0:T(1024)(128)(4,1)S(1)}, s32[]{:S(2)}) async-start(s8[9437184]{0:T(1024)(128)(4,1)} %bitcast.39), calls=%async_computation.7 | async-start | bytes 2097152
  145.8 14.0 %copy-start.6 = (f32[16,2]{0,1:T(2,128)S(1)}, f32[16,2]{0,1:T(2,128)}, u32[]{:S(2)}) copy-start(f32[16,2]{0,1:T(2,128)} %param.24) | copy-start | bytes 388
  154.0 32.0 %all-to-all-start.1 = ((f32[8,16,2048]{2,1,0:T(8,128)}), f32[8,16,2048]{2,1,0:T(8,128)S(1)}, u32[]{:S(2)}, u32[]{:S(2)}) async-start(f32[8,16,2048]{2,1,0:T(8,128)} %fusion.2), calls=%async_computation.2 | async-start | bytes 2097152 | tf_op jit(solution)/shard_map/all_to_all | solution.py:90
  159.8 26.3 %copy-start.1 = (f32[16,2048]{1,0:T(8,128)S(1)}, f32[16,2048]{1,0:T(8,128)}, u32[]{:S(2)}) copy-start(f32[16,2048]{1,0:T(8,128)} %reduce-scatter.2.cloned.1.call-done) | copy-start | bytes 393220
Sparse Core Ops, SparseCore 0:
  32.2 66.1 reduce-scatter.1
  125.1 20.7 all-reduce.2
where the time goes:
time: 196 us; the launch traced here: 195 us
  waiting for transfers between devices  102 us (52%)
  matrix products  37.5 us (19%)
  blocking collectives  20.9 us (11%)
  between operations  14.2 us (7%)
  other arithmetic  12.6 us (6%)
  starting transfers between devices  5.84 us (3%)
  local copies, waits for them, and re-layouts  2.27 us (1%)
    reduce_scatter x1, waiting for transfers between devices, shards(): lax.psum_scatter(jnp.dot(all_heads, out_proj, preferred_element_type=jnp....  65.9 us
    psum x1, waiting for transfers between devices, shards(): lax.psum((gate_part, up_part, squares), ('tp', 'sub'))  18.2 us
    dot_general x1, matrix products, shards(): jnp.einsum('rhi,rhij->rhj', query_heads, updated, precision=lax.Precision...  17.8 us
    all_to_all x1, waiting for transfers between devices, shards(): lax.all_to_all(expert_out, 'dev', split_axis=0, concat_axis=0, tiled=True)  17.6 us
    all_to_all x1, blocking collectives, shards(): lax.all_to_all(outgoing, 'dev', split_axis=0, concat_axis=0, tiled=True)  16.3 us
    convert_element_type x1, other arithmetic, shards(): new_states = updated.astype(jnp.bfloat16)  8.56 us
    dot_general x1, matrix products, shards(): up_part = jnp.dot(scaled, expert_up[0], preferred_element_type=jnp.float32)  6.28 us
    dot_general x1, matrix products, shards(): produced = jnp.dot(act, expert_down[0], preferred_element_type=jnp.float32)  6.15 us
  transfers between devices with their start and end apart: 3, of which 3 were waited for; matrix products, arithmetic and copies ran while one was open for 5% of the time, Pallas kernels for 0%

commit v1 on v0

--- a/solution.py
+++ b/solution.py
@@ -1,6 +1,8 @@
 import jax
 import jax.numpy as jnp
 from jax import lax
+from jax.experimental import pallas as pl
+from jax.experimental.pallas import tpu as pltpu
 from jax.sharding import PartitionSpec as P
 
 D = 4096
@@ -95,7 +97,336 @@
     return (mixed, new_states)
 
 
+ROWS = 16
+HEAD_STEP = 2
+PIECES = 4
+TILE = 256
+MESH = pl.DeviceIdType.MESH
+
+
+def state_kernel(q_ref, k_ref, v_ref, g_ref, s_ref, d_ref, new_ref, out_ref):
+    rows, heads, size = s_ref.shape[0], s_ref.shape[1], s_ref.shape[3]
+    row_ids = lax.broadcasted_iota(jnp.int32, (rows, size), 0)
+    for h in range(heads):
+        lanes = pl.ds(h * size, size)
+        q = q_ref[:, lanes]
+        q32 = q.astype(jnp.float32)
+        k32 = k_ref[:, lanes].astype(jnp.float32)
+        v32 = v_ref[:, lanes].astype(jnp.float32)
+        columns = k32.T
+        retain = jnp.exp(-d_ref[h])
+        read = jnp.zeros((rows, size), jnp.float32)
+        for r in range(rows):
+            state = s_ref[r, h]
+            product = jnp.dot(q, state, preferred_element_type=jnp.float32)
+            read = jnp.where(row_ids == r, product, read)
+            new_ref[r, h] = (
+                retain * state.astype(jnp.float32) + columns[:, r : r + 1] * v32[r : r + 1, :]
+            ).astype(jnp.bfloat16)
+        overlap = jnp.sum(q32 * k32, axis=1, keepdims=True)
+        read = (retain * read + overlap * v32) * size ** (-0.5)
+        gate = g_ref[:, lanes].astype(jnp.float32)
+        out_ref[:, lanes] = (read / (1.0 + jnp.exp(-gate))).astype(jnp.bfloat16)
+
+
+def update_states(new_query, new_key, new_value, out_gate, states, decay_rate):
+    reqs, heads, size = states.shape[0], states.shape[1], states.shape[3]
+    flat = pl.BlockSpec((ROWS, HEAD_STEP * size), lambda i, j: (i, j))
+    block = pl.BlockSpec((ROWS, HEAD_STEP, size, size), lambda i, j: (i, j, 0, 0))
+    return pl.pallas_call(
+        state_kernel,
+        grid=(reqs // ROWS, heads // HEAD_STEP),
+        in_specs=[flat, flat, flat, flat, block, pl.BlockSpec((HEAD_STEP, 1, 1), lambda i, j: (j, 0, 0))],
+        out_specs=[block, flat],
+        out_shape=[
+            jax.ShapeDtypeStruct(states.shape, jnp.bfloat16),
+            jax.ShapeDtypeStruct((reqs, heads * size), jnp.bfloat16),
+        ],
+        compiler_params=pltpu.CompilerParams(vmem_limit_bytes=40 * 2**20),
+        name="states",
+    )(new_query, new_key, new_value, out_gate, states, decay_rate.reshape(heads, 1, 1))
+
+
+def send(src, dst, send_sem, recv_sem, **target):
+    return pltpu.make_async_remote_copy(
+        src_ref=src,
+        dst_ref=dst,
+        send_sem=send_sem,
+        recv_sem=recv_sem,
+        device_id=target,
+        device_id_type=MESH,
+    )
+
+
+def layer_kernel(
+    head_ref, hidden_ref, gain_ref, routes_ref, weight_ref, proj_hbm, gate_hbm, up_hbm, down_hbm,
+    mixed_ref,
+    proj, gate, up, down, load_sem,
+    heads, coeffs, rows, own, scaled, inverse, act,
+    part32, part16, from_x, sum32, sum16, from_z,
+    head_sem, coeff_z_sem, coeff_x_sem, rows_z_sem, rows_x_sem, x_sem, z_sem,
+    hidden32, hidden16, hidden_in, hidden_sem, square_own, square_in, square_sem,
+):
+    sub = lax.axis_index("sub")
+    dev = lax.axis_index("dev")
+    z, x = dev // 2, dev % 2
+    sibling, across = 1 - sub, z * 2 + (1 - x)
+    width = rows.shape[2]
+    half = head_ref.shape[0]
+
+    loads = []
+    for src, dst, parts in ((proj_hbm, proj, 1), (gate_hbm.at[0], gate, 4), (up_hbm.at[0], up, 4), (down_hbm.at[0], down, 4)):
+        depth = dst.shape[0] // parts
+        for p in range(parts):
+            span = pl.ds(p * depth, depth)
+            loads.append(pltpu.make_async_copy(src.at[span], dst.at[span], load_sem.at[len(loads)]))
+    for load in loads:
+        load.start()
+
+    barrier = pltpu.get_barrier_semaphore()
+    pl.semaphore_signal(barrier, inc=1, device_id={"sub": sibling}, device_id_type=MESH)
+    pl.semaphore_signal(barrier, inc=1, device_id={"dev": across}, device_id_type=MESH)
+    for dz in (1, 2, 3):
+        pl.semaphore_signal(barrier, inc=1, device_id={"dev": (z + dz) % 4 * 2 + x}, device_id_type=MESH)
+    pl.semaphore_wait(barrier, 5)
+
+    def head_copy(who):
+        return send(head_ref, heads.at[pl.ds(pl.multiple_of(who * half, half), half)], head_sem.at[0], head_sem.at[1], sub=sibling)
+
+    head_copy(sub).start()
+    heads[pl.ds(pl.multiple_of(sub * half, half), half), :] = head_ref[...]
+
+    def block(buffer, owner):
+        return buffer.at[pl.ds(pl.multiple_of(owner * ROWS, ROWS), ROWS)]
+
+    def gather_z(buffer, sems, dz, owner_z):
+        place = block(buffer, owner_z * 2 + x)
+        return send(place, place, sems.at[0, dz - 1], sems.at[1, dz - 1], dev=(z + dz) % 4 * 2 + x)
+
+    def gather_x(buffer, sems, dz, owner_x):
+        place = block(buffer, (z - dz + 4) % 4 * 2 + owner_x)
+        return send(place, place, sems.at[0, dz], sems.at[1, dz], dev=across)
+
+    def gather_start(buffer, z_sems, x_sems):
+        for dz in (2, 1, 3):
+            gather_z(buffer, z_sems, dz, z).start()
+        gather_x(buffer, x_sems, 0, x).start()
+
+    def gather_forward(buffer, z_sems, x_sems):
+        for dz in (1, 3, 2):
+            gather_z(buffer, z_sems, dz, (z - dz + 4) % 4).wait_recv()
+            gather_x(buffer, x_sems, dz, x).start()
+
+    def gather_finish(buffer, z_sems, x_sems):
+        for dz in (0, 1, 3, 2):
+            gather_x(buffer, x_sems, dz, 1 - x).wait_recv()
+            gather_x(buffer, x_sems, dz, x).wait_send()
+        for dz in (1, 2, 3):
+            gather_z(buffer, z_sems, dz, z).wait_send()
+
+    lane = lax.broadcasted_iota(jnp.int32, (ROWS, 128), 1)
+    table = jnp.zeros((ROWS, 128), jnp.float32)
+    for j in range(routes_ref.shape[1]):
+        table = table + jnp.where(lane == routes_ref[:, j : j + 1], weight_ref[:, j : j + 1], 0.0)
+    coeffs[pl.ds(pl.multiple_of(dev * ROWS, ROWS), ROWS), :] = table
+    gather_start(coeffs, coeff_z_sem, coeff_x_sem)
+
+    def reduce_x(turn, c):
+        return send(part16.at[turn, c, 1 - x], from_x.at[turn, c], x_sem.at[turn, 0, c], x_sem.at[turn, 1, c], dev=across)
+
+    def reduce_z(turn, c, dz):
+        there = (z + dz) % 4
+        return send(sum16.at[turn, c, there], from_z.at[turn, c, dz - 1], z_sem.at[turn, 0, c, dz - 1], z_sem.at[turn, 1, c, dz - 1], dev=there * 2 + x)
+
+    def reduce_start(turn, c, value):
+        for d in range(2 * part32.shape[3]):
+            piece = value[d * ROWS : (d + 1) * ROWS]
+            part32[turn, c, d % 2, d // 2] = piece
+            part16[turn, c, d % 2, d // 2] = piece.astype(jnp.bfloat16)
+        reduce_x(turn, c).start()
+
+    def reduce_forward(turn, c):
+        reduce_x(turn, c).wait_recv()
+        total = part32[turn, c, x] + from_x[turn, c].astype(jnp.float32)
+        sum32[turn, c] = total
+        sum16[turn, c] = total.astype(jnp.bfloat16)
+        for dz in (2, 1, 3):
+            reduce_z(turn, c, dz).start()
+
+    def reduce_finish(turn, c):
+        total = sum32[turn, c, z]
+        for dz in (1, 3, 2):
+            reduce_z(turn, c, dz).wait_recv()
+            total = total + from_z[turn, c, dz - 1].astype(jnp.float32)
+        return total
+
+    def each(count, body):
+        def step(i, carry):
+            body(i)
+            return carry
+
+        lax.fori_loop(0, count, step, 0)
+
+    def columns(c, size):
+        return pl.ds(pl.multiple_of(c * size, size), size)
+
+    loads[0].wait()
+    head_copy(sibling).wait_recv()
+
+    def project(c):
+        reduce_start(0, c, jnp.dot(heads[...], proj[:, columns(c, width)], preferred_element_type=jnp.float32))
+
+    each(PIECES, project)
+    gather_forward(coeffs, coeff_z_sem, coeff_x_sem)
+    each(PIECES, lambda c: reduce_forward(0, c))
+
+    def settle(c):
+        lanes = columns(c, width)
+        residual = (hidden_ref[:, lanes].astype(jnp.float32) + reduce_finish(0, c)).astype(jnp.bfloat16)
+        own[:, lanes] = residual
+        rows[c, pl.ds(pl.multiple_of(dev * ROWS, ROWS), ROWS), :] = residual
+        gather_start(rows.at[c], rows_z_sem.at[c], rows_x_sem.at[c])
+
+    each(PIECES, settle)
+    each(PIECES, lambda c: gather_forward(rows.at[c], rows_z_sem.at[c], rows_x_sem.at[c]))
+    square_own[...] = jnp.zeros_like(square_own)
+
+    def scale(c):
+        gather_finish(rows.at[c], rows_z_sem.at[c], rows_x_sem.at[c])
+        lanes = columns(c, width)
+        value = rows[c].astype(jnp.float32)
+        scaled[:, lanes] = (value * gain_ref[:, lanes]).astype(jnp.bfloat16)
+        square_own[...] += jnp.broadcast_to(jnp.sum(value * value, axis=1, keepdims=True), square_own.shape)
+
+    each(PIECES, scale)
+    square_copy = send(square_own, square_in, square_sem.at[0], square_sem.at[1], sub=sibling)
+    square_copy.start()
+    for load in loads[1:9]:
+        load.wait()
+
+    def hidden_copy(t):
+        return send(hidden16.at[t], hidden_in.at[t], hidden_sem.at[0, t], hidden_sem.at[1, t], sub=sibling)
+
+    tiles = gate.shape[1] // TILE
+
+    def enter(t):
+        lanes = columns(t, TILE)
+        for j, weights in enumerate((gate, up)):
+            value = jnp.dot(scaled[...], weights[:, lanes], preferred_element_type=jnp.float32)
+            hidden32[t, j] = value
+            hidden16[t, j] = value.astype(jnp.bfloat16)
+        hidden_copy(t).start()
+
+    each(tiles, enter)
+    square_copy.wait_recv()
+    inverse[...] = lax.rsqrt((square_own[...] + square_in[...]) / D + EPS)
+    gather_finish(coeffs, coeff_z_sem, coeff_x_sem)
+
+    def activate(t):
+        hidden_copy(t).wait_recv()
+        factor = inverse[:, :1]
+        opened = factor * (hidden32[t, 0] + hidden_in[t, 0].astype(jnp.float32))
+        raised = factor * (hidden32[t, 1] + hidden_in[t, 1].astype(jnp.float32))
+        act[:, columns(t, TILE)] = (opened / (1.0 + jnp.exp(-opened)) * raised).astype(jnp.bfloat16)
+
+    each(tiles, activate)
+    for load in loads[9:]:
+        load.wait()
+
+    def leave(c):
+        mine = lax.broadcasted_iota(jnp.int32, coeffs.shape, 1) == z
+        factor = jnp.sum(jnp.where(mine, coeffs[...], 0.0), axis=1, keepdims=True)
+        produced = jnp.dot(act[...], down[:, columns(c, width)], preferred_element_type=jnp.float32)
+        reduce_start(1, c, factor * produced)
+
+    each(PIECES, leave)
+    each(PIECES, lambda c: reduce_forward(1, c))
+
+    def close(c):
+        lanes = columns(c, width)
+        mixed_ref[:, lanes] = (own[:, lanes].astype(jnp.float32) + reduce_finish(1, c)).astype(jnp.bfloat16)
+
+    each(PIECES, close)
+    head_copy(sub).wait_send()
+    square_copy.wait_send()
+    each(tiles, lambda t: hidden_copy(t).wait_send())
+
+    def drain(c):
+        for turn in range(2):
+            reduce_x(turn, c).wait_send()
+            for dz in (1, 2, 3):
+                reduce_z(turn, c, dz).wait_send()
+
+    each(PIECES, drain)
+
+
+def run_layer(head_out, hidden, norm_gain, routes, route_weight, out_proj, expert_gate, expert_up, expert_down):
+    depth, features = out_proj.shape
+    inner = expert_gate.shape[2]
+    reqs = 8 * ROWS
+    width = features // PIECES
+    tiles = inner // TILE
+    vmem = pl.BlockSpec(memory_space=pltpu.VMEM)
+    anywhere = pl.BlockSpec(memory_space=pl.ANY)
+    bf16, f32, dma = jnp.bfloat16, jnp.float32, pltpu.SemaphoreType.DMA
+    return pl.pallas_call(
+        layer_kernel,
+        in_specs=[vmem] * 5 + [anywhere] * 4,
+        out_specs=vmem,
+        out_shape=jax.ShapeDtypeStruct(hidden.shape, bf16),
+        scratch_shapes=[
+            pltpu.VMEM((depth, features), bf16),
+            pltpu.VMEM((features, inner), bf16),
+            pltpu.VMEM((features, inner), bf16),
+            pltpu.VMEM((inner, features), bf16),
+            dma((13,)),
+            pltpu.VMEM((reqs, depth), bf16),
+            pltpu.VMEM((reqs, 128), f32),
+            pltpu.VMEM((PIECES, reqs, width), bf16),
+            pltpu.VMEM((ROWS, features), bf16),
+            pltpu.VMEM((reqs, features), bf16),
+            pltpu.VMEM((reqs, 128), f32),
+            pltpu.VMEM((reqs, inner), bf16),
+            pltpu.VMEM((2, PIECES, 2, 4, ROWS, width), f32),
+            pltpu.VMEM((2, PIECES, 2, 4, ROWS, width), bf16),
+            pltpu.VMEM((2, PIECES, 4, ROWS, width), bf16),
+            pltpu.VMEM((2, PIECES, 4, ROWS, width), f32),
+            pltpu.VMEM((2, PIECES, 4, ROWS, width), bf16),
+            pltpu.VMEM((2, PIECES, 3, ROWS, width), bf16),
+            dma((2,)),
+            dma((2, 3)),
+            dma((2, 4)),
+            dma((PIECES, 2, 3)),
+            dma((PIECES, 2, 4)),
+            dma((2, 2, PIECES)),
+            dma((2, 2, PIECES, 3)),
+            pltpu.VMEM((tiles, 2, reqs, TILE), f32),
+            pltpu.VMEM((tiles, 2, reqs, TILE), bf16),
+            pltpu.VMEM((tiles, 2, reqs, TILE), bf16),
+            dma((2, tiles)),
+            pltpu.VMEM((reqs, 128), f32),
+            pltpu.VMEM((reqs, 128), f32),
+            dma((2,)),
+        ],
+        compiler_params=pltpu.CompilerParams(
+            collective_id=0, has_side_effects=True, vmem_limit_bytes=58 * 2**20
+        ),
+        name="layer",
+    )(head_out, hidden, norm_gain.reshape(1, features), routes, route_weight, out_proj, expert_gate, expert_up, expert_down)
+
+
+def fused_shards(
+    hidden, new_query, new_key, new_value, out_gate, states, decay_rate, out_proj, norm_gain,
+    routes, route_weight, expert_gate, expert_up, expert_down,
+):
+    new_states, head_out = update_states(new_query, new_key, new_value, out_gate, states, decay_rate)
+    mixed = run_layer(head_out, hidden, norm_gain, routes, route_weight, out_proj, expert_gate, expert_up, expert_down)
+    return (mixed, new_states)
+
+
 def solution(mesh):
+    sizes = dict(mesh.shape)
+    fits = sizes["dev"] == 8 and sizes["tp"] == 1 and sizes["sub"] == 2
     placed = (
         P(("groups", "dev"), ("tp", "sub")),
         P(("groups", "tp", "sub"), "dev"),
@@ -113,7 +444,7 @@
         P("dev", None, ("tp", "sub")),
     )
     return jax.shard_map(
-        shards,
+        fused_shards if fits else shards,
         mesh=mesh,
         in_specs=placed,
         out_specs=(

time: 196 us -> 68.5 us (0.35)
  waiting for transfers between devices: 102 us -> 0 us
  Pallas kernels: 0 us -> 55.1 us
  matrix products: 37.5 us -> 0 us
  blocking collectives: 20.9 us -> 0 us
  between operations: 14.2 us -> 0.65 us
  other arithmetic: 12.6 us -> 0 us
  local copies, waits for them, and re-layouts: 2.27 us -> 12.3 us
  starting transfers between devices: 5.84 us -> 0 us
    reduce_scatter x1 -> x0, waiting for transfers between devices: 65.9 us -> none  [shards(): lax.psum_scatter(jnp.dot(all_heads, out_proj, preferred_element_type=jnp....]
    pallas_call x0 -> x2, Pallas kernels: none -> 55.1 us  [the longest x1 47.3 us: run_layer(): pl.pallas_call(layer_kernel, in_specs=[vmem] * 5 + [anywhere] * 4, out_sp...]
    dot_general x7 -> x0, matrix products: 37.5 us -> none  [the longest x1 17.8 us: shards(): jnp.einsum('rhi,rhij->rhj', query_heads, updated, precision=lax.Precision...]
    psum x1 -> x0, waiting for transfers between devices: 18.2 us -> none  [shards(): lax.psum((gate_part, up_part, squares), ('tp', 'sub'))]
    all_to_all x1 -> x0, waiting for transfers between devices: 17.6 us -> none  [shards(): lax.all_to_all(expert_out, 'dev', split_axis=0, concat_axis=0, tiled=True)]
    all_to_all x1 -> x0, blocking collectives: 16.3 us -> none  [shards(): lax.all_to_all(outgoing, 'dev', split_axis=0, concat_axis=0, tiled=True)]
    unnamed x20 -> x15, local copies, waits for them, and re-layouts: 0.05 us -> 11.5 us
    convert_element_type x3 -> x0, other arithmetic: 10.6 us -> none  [the longest x1 8.56 us: shards(): new_states = updated.astype(jnp.bfloat16)]
  transfers between devices with their start and end apart: 3 -> 0, of which waited for: 3 -> 0; matrix products, arithmetic and copies ran while one was open for 5% -> 0% of each run, Pallas kernels for 0% -> 0%
where the time goes in v1:
time: 68.5 us; the launch traced here: 68.1 us
  Pallas kernels  55.1 us (80%)
  local copies, waits for them, and re-layouts  12.3 us (18%)
    pallas_call x1, Pallas kernels, run_layer(): pl.pallas_call(layer_kernel, in_specs=[vmem] * 5 + [anywhere] * 4, out_sp...  47.3 us
    unnamed x15, local copies, waits for them, and re-layouts  11.5 us
    pallas_call x1, Pallas kernels, update_states(): pl.pallas_call(state_kernel, grid=(reqs // ROWS, heads // HEAD_STEP), in_...  7.8 us

profile of v1, /device:TPU:0, one launch (start us, length us, event | category | flops | bytes accessed | tf_op | source)
XLA Modules:
  0.0 68.1 jit_solution(4125943390208257662)
XLA Ops:
  0.6 0.7 %copy.16.d_ref = f32[4,1,1]{2,1,0:T(1,128)S(1)} copy(f32[4,1,1]{0,2,1:T(1,128)} %bitcast.3) | data formatting | bytes 32 | tf_op jit(solution)/shard_map/reshape | solution.py:147
  1.4 1.3 %copy.17.routes_ref = s32[16,2]{1,0:T(8,128)} copy(s32[16,2]{0,1:T(2,128)} %param.23) | data formatting | bytes 256 | tf_op args[9]
  2.7 1.3 %copy.18.weight_ref = f32[16,2]{1,0:T(8,128)} copy(f32[16,2]{0,1:T(2,128)} %param.24) | data formatting | bytes 256 | tf_op args[10]
  4.1 0.0 copy-start
  4.1 3.4 %copy-done = bf16[64,4,128,128]{3,2,1,0:T(8,128)(2,1)S(1)} copy-done((bf16[64,4,128,128]{3,2,1,0:T(8,128)(2,1)S(1)}, bf16[64,4,128,128]{3,2,1,0:T(8,128)(2,1)}, u32[]{:S(2)}) %copy-start) | copy-done | bytes 8388632
  7.4 0.0 copy-start.1
  7.4 0.8 %copy-done.1 = bf16[64,512]{1,0:T(8,128)(2,1)S(1)} copy-done((bf16[64,512]{1,0:T(8,128)(2,1)S(1)}, bf16[64,512]{1,0:T(8,128)(2,1)}, u32[]{:S(2)}) %copy-start.1) | copy-done | bytes 65560
  8.3 0.0 copy-start.2
  8.3 0.8 %copy-done.2 = bf16[64,512]{1,0:T(8,128)(2,1)S(1)} copy-done((bf16[64,512]{1,0:T(8,128)(2,1)S(1)}, bf16[64,512]{1,0:T(8,128)(2,1)}, u32[]{:S(2)}) %copy-start.2) | copy-done | bytes 65560
  9.1 0.0 copy-start.3
  9.1 0.8 %copy-done.3 = bf16[64,512]{1,0:T(8,128)(2,1)S(1)} copy-done((bf16[64,512]{1,0:T(8,128)(2,1)S(1)}, bf16[64,512]{1,0:T(8,128)(2,1)}, u32[]{:S(2)}) %copy-start.3) | copy-done | bytes 65560
  10.0 0.0 copy-start.4
  10.0 0.8 %copy-done.4 = bf16[64,512]{1,0:T(8,128)(2,1)S(1)} copy-done((bf16[64,512]{1,0:T(8,128)(2,1)S(1)}, bf16[64,512]{1,0:T(8,128)(2,1)}, u32[]{:S(2)}) %copy-start.4) | copy-done | bytes 65560
  10.8 7.8 %states.1 = (bf16[64,4,128,128]{3,2,1,0:T(8,128)(2,1)}, bf16[64,512]{1,0:T(8,128)(2,1)S(1)}) custom-call(bf16[64,512]{1,0:T(8,128)(2,1)S(1)} %copy-done.1, bf16[64,512]{1,0:T(8,128)(2,1)S(1)} %copy-done.2, bf16[64,512]{1,0:T(8,128)(2,1)S(1)} %copy-done.3, bf16[64,512]{1,0:T(8,128)(2,1)S(1)} %copy-done.4, bf16[64,4,128,128]{3,2,1,0:T(8,128)(2,1)S(1)} %copy-done, ...), custom_call_target="tpu_custom_call" | custom-call | tf_op jit(solution)/shard_map/states/pallas_call | solution.py:136
  18.6 0.0 copy-start.5
  18.6 0.6 copy-done.5
  19.2 47.3 %layer.1 = bf16[16,2048]{1,0:T(8,128)(2,1)} custom-call(bf16[64,512]{1,0:T(8,128)(2,1)} %copy-done.5, bf16[16,2048]{1,0:T(8,128)(2,1)} %hidden_ref.1, f32[1,2048]{1,0:T(1,128)} %bitcast.2, s32[16,2]{1,0:T(8,128)} %copy.17.routes_ref, f32[16,2]{1,0:T(8,128)} %copy.18.weight_ref, bf16[512,2048]{1,0:T(8,128)(2,1)} %proj_hbm.1, bf16[1,2048,2304]{2,1,0:T(8,128)(2,1)} %gate_hbm.1, ...), custom_call_target="tpu_custom_call" | custom-call | tf_op jit(solution)/shard_map/layer/pallas_call | solution.py:372
  66.6 1.5 %copy.20 = bf16[16,2048]{1,0:T(8,128)(2,1)} copy(bf16[16,2048]{1,0:T(8,128)(2,1)} %layer.1) | data formatting | bytes 131072
Async XLA Ops:
  4.1 3.4 %copy-start = (bf16[64,4,128,128]{3,2,1,0:T(8,128)(2,1)S(1)}, bf16[64,4,128,128]{3,2,1,0:T(8,128)(2,1)}, u32[]{:S(2)}) copy-start(bf16[64,4,128,128]{3,2,1,0:T(8,128)(2,1)} %s_ref.1) | copy-start | bytes 25165828
  7.4 0.8 %copy-start.1 = (bf16[64,512]{1,0:T(8,128)(2,1)S(1)}, bf16[64,512]{1,0:T(8,128)(2,1)}, u32[]{:S(2)}) copy-start(bf16[64,512]{1,0:T(8,128)(2,1)} %q_ref.1) | copy-start | bytes 196612
  8.3 0.8 %copy-start.2 = (bf16[64,512]{1,0:T(8,128)(2,1)S(1)}, bf16[64,512]{1,0:T(8,128)(2,1)}, u32[]{:S(2)}) copy-start(bf16[64,512]{1,0:T(8,128)(2,1)} %k_ref.1) | copy-start | bytes 196612
  9.1 0.8 %copy-start.3 = (bf16[64,512]{1,0:T(8,128)(2,1)S(1)}, bf16[64,512]{1,0:T(8,128)(2,1)}, u32[]{:S(2)}) copy-start(bf16[64,512]{1,0:T(8,128)(2,1)} %v_ref.1) | copy-start | bytes 196612
  10.0 0.8 %copy-start.4 = (bf16[64,512]{1,0:T(8,128)(2,1)S(1)}, bf16[64,512]{1,0:T(8,128)(2,1)}, u32[]{:S(2)}) copy-start(bf16[64,512]{1,0:T(8,128)(2,1)} %g_ref.1) | copy-start | bytes 196612
  18.6 0.6 copy-start.5

commit v2 on v1

--- a/solution.py
+++ b/solution.py
@@ -98,53 +98,87 @@
 
 
 ROWS = 16
-HEAD_STEP = 2
+COPIES = 4
 PIECES = 4
 TILE = 256
 MESH = pl.DeviceIdType.MESH
 
 
-def state_kernel(q_ref, k_ref, v_ref, g_ref, s_ref, d_ref, new_ref, out_ref):
-    rows, heads, size = s_ref.shape[0], s_ref.shape[1], s_ref.shape[3]
-    row_ids = lax.broadcasted_iota(jnp.int32, (rows, size), 0)
-    for h in range(heads):
-        lanes = pl.ds(h * size, size)
-        q = q_ref[:, lanes]
-        q32 = q.astype(jnp.float32)
-        k32 = k_ref[:, lanes].astype(jnp.float32)
-        v32 = v_ref[:, lanes].astype(jnp.float32)
-        columns = k32.T
-        retain = jnp.exp(-d_ref[h])
-        read = jnp.zeros((rows, size), jnp.float32)
-        for r in range(rows):
-            state = s_ref[r, h]
-            product = jnp.dot(q, state, preferred_element_type=jnp.float32)
-            read = jnp.where(row_ids == r, product, read)
-            new_ref[r, h] = (
-                retain * state.astype(jnp.float32) + columns[:, r : r + 1] * v32[r : r + 1, :]
-            ).astype(jnp.bfloat16)
-        overlap = jnp.sum(q32 * k32, axis=1, keepdims=True)
-        read = (retain * read + overlap * v32) * size ** (-0.5)
-        gate = g_ref[:, lanes].astype(jnp.float32)
-        out_ref[:, lanes] = (read / (1.0 + jnp.exp(-gate))).astype(jnp.bfloat16)
+def state_kernel(q_ref, k_ref, v_ref, g_ref, d_ref, s_hbm, new_hbm, out_ref, old, new, in_sem, out_sem):
+    reqs, heads, size = old.shape[0], old.shape[1], old.shape[3]
+    steps = reqs // ROWS
+    row_ids = lax.broadcasted_iota(jnp.int32, (ROWS, size), 0)
+    part = ROWS // COPIES
+
+    def span(i, p):
+        return pl.ds(i * ROWS + p * part, part)
+
+    def load(i, p):
+        return pltpu.make_async_copy(s_hbm.at[span(i, p)], old.at[span(i, p)], in_sem.at[i, p])
+
+    def store(i, p):
+        return pltpu.make_async_copy(new.at[span(i, p)], new_hbm.at[span(i, p)], out_sem.at[i, p])
+
+    for i in range(steps):
+        for p in range(COPIES):
+            load(i, p).start()
+
+    def step(i, carry):
+        here = pl.ds(pl.multiple_of(i * ROWS, ROWS), ROWS)
+        for p in range(COPIES):
+            load(i, p).wait()
+        for h in range(heads):
+            lanes = slice(h * size, (h + 1) * size)
+            q = q_ref[here, lanes]
+            q32 = q.astype(jnp.float32)
+            k32 = k_ref[here, lanes].astype(jnp.float32)
+            v32 = v_ref[here, lanes].astype(jnp.float32)
+            columns = k32.T.astype(jnp.bfloat16)
+            retain = jnp.exp(-d_ref[:, h : h + 1])
+            read = jnp.zeros((ROWS, size), jnp.float32)
+            for r in range(ROWS):
+                state = old[i * ROWS + r, h]
+                product = jnp.dot(q, state, preferred_element_type=jnp.float32)
+                read = jnp.where(row_ids == r, product, read)
+                only = jnp.where(row_ids == r, v32, 0.0).astype(jnp.bfloat16)
+                outer = jnp.dot(columns, only, preferred_element_type=jnp.float32)
+                new[i * ROWS + r, h] = (retain * state.astype(jnp.float32) + outer).astype(jnp.bfloat16)
+            overlap = jnp.sum(q32 * k32, axis=1, keepdims=True)
+            read = (retain * read + overlap * v32) * size ** (-0.5)
+            gate = g_ref[here, lanes].astype(jnp.float32)
+            out_ref[here, lanes] = (read / (1.0 + jnp.exp(-gate))).astype(jnp.bfloat16)
+        for p in range(COPIES):
+            store(i, p).start()
+        return carry
+
+    lax.fori_loop(0, steps, step, 0)
+    for i in range(steps):
+        for p in range(COPIES):
+            store(i, p).wait()
 
 
 def update_states(new_query, new_key, new_value, out_gate, states, decay_rate):
     reqs, heads, size = states.shape[0], states.shape[1], states.shape[3]
-    flat = pl.BlockSpec((ROWS, HEAD_STEP * size), lambda i, j: (i, j))
-    block = pl.BlockSpec((ROWS, HEAD_STEP, size, size), lambda i, j: (i, j, 0, 0))
+    vmem = pl.BlockSpec(memory_space=pltpu.VMEM)
+    anywhere = pl.BlockSpec(memory_space=pl.ANY)
+    sems = pltpu.SemaphoreType.DMA((reqs // ROWS, COPIES))
     return pl.pallas_call(
         state_kernel,
-        grid=(reqs // ROWS, heads // HEAD_STEP),
-        in_specs=[flat, flat, flat, flat, block, pl.BlockSpec((HEAD_STEP, 1, 1), lambda i, j: (j, 0, 0))],
-        out_specs=[block, flat],
+        in_specs=[vmem] * 5 + [anywhere],
+        out_specs=[anywhere, vmem],
         out_shape=[
             jax.ShapeDtypeStruct(states.shape, jnp.bfloat16),
             jax.ShapeDtypeStruct((reqs, heads * size), jnp.bfloat16),
         ],
-        compiler_params=pltpu.CompilerParams(vmem_limit_bytes=40 * 2**20),
+        scratch_shapes=[
+            pltpu.VMEM(states.shape, jnp.bfloat16),
+            pltpu.VMEM(states.shape, jnp.bfloat16),
+            sems,
+            sems,
+        ],
+        compiler_params=pltpu.CompilerParams(vmem_limit_bytes=60 * 2**20),
         name="states",
-    )(new_query, new_key, new_value, out_gate, states, decay_rate.reshape(heads, 1, 1))
+    )(new_query, new_key, new_value, out_gate, decay_rate.reshape(1, heads), states)
 
 
 def send(src, dst, send_sem, recv_sem, **target):
@@ -226,8 +260,14 @@
 
     lane = lax.broadcasted_iota(jnp.int32, (ROWS, 128), 1)
     table = jnp.zeros((ROWS, 128), jnp.float32)
-    for j in range(routes_ref.shape[1]):
-        table = table + jnp.where(lane == routes_ref[:, j : j + 1], weight_ref[:, j : j + 1], 0.0)
+    square = (ROWS, ROWS)
+    diagonal = lax.broadcasted_iota(jnp.int32, square, 0) == lax.broadcasted_iota(jnp.int32, square, 1)
+    for j in range(routes_ref.shape[0]):
+        chosen = jnp.broadcast_to(routes_ref[j : j + 1, :].astype(jnp.float32), square)
+        chosen = jnp.sum(jnp.where(diagonal, chosen, 0.0), axis=1, keepdims=True)
+        share = jnp.broadcast_to(weight_ref[j : j + 1, :], square)
+        share = jnp.sum(jnp.where(diagonal, share, 0.0), axis=1, keepdims=True)
+        table = table + jnp.where(lane == chosen.astype(jnp.int32), share, 0.0)
     coeffs[pl.ds(pl.multiple_of(dev * ROWS, ROWS), ROWS), :] = table
     gather_start(coeffs, coeff_z_sem, coeff_x_sem)
 
@@ -298,21 +338,30 @@
         scaled[:, lanes] = (value * gain_ref[:, lanes]).astype(jnp.bfloat16)
         square_own[...] += jnp.broadcast_to(jnp.sum(value * value, axis=1, keepdims=True), square_own.shape)
 
-    each(PIECES, scale)
+    early = PIECES // 2
+    split = early * width
+    tiles = gate.shape[1] // TILE
+    each(early, scale)
+    for load in loads[1:9]:
+        load.wait()
+
+    def begin(t):
+        lanes = columns(t, TILE)
+        for j, weights in enumerate((gate, up)):
+            hidden32[t, j] = jnp.dot(scaled[:, :split], weights[:split, lanes], preferred_element_type=jnp.float32)
+
+    each(tiles, begin)
+    each(PIECES - early, lambda c: scale(c + early))
     square_copy = send(square_own, square_in, square_sem.at[0], square_sem.at[1], sub=sibling)
     square_copy.start()
-    for load in loads[1:9]:
-        load.wait()
 
     def hidden_copy(t):
         return send(hidden16.at[t], hidden_in.at[t], hidden_sem.at[0, t], hidden_sem.at[1, t], sub=sibling)
-
-    tiles = gate.shape[1] // TILE
 
     def enter(t):
         lanes = columns(t, TILE)
         for j, weights in enumerate((gate, up)):
-            value = jnp.dot(scaled[...], weights[:, lanes], preferred_element_type=jnp.float32)
+            value = hidden32[t, j] + jnp.dot(scaled[:, split:], weights[split:, lanes], preferred_element_type=jnp.float32)
             hidden32[t, j] = value
             hidden16[t, j] = value.astype(jnp.bfloat16)
         hidden_copy(t).start()
@@ -412,7 +461,7 @@
             collective_id=0, has_side_effects=True, vmem_limit_bytes=58 * 2**20
         ),
         name="layer",
-    )(head_out, hidden, norm_gain.reshape(1, features), routes, route_weight, out_proj, expert_gate, expert_up, expert_down)
+    )(head_out, hidden, norm_gain.reshape(1, features), routes.T, route_weight.T, out_proj, expert_gate, expert_up, expert_down)
 
 
 def fused_shards(

time: 68.5 us -> 57.7 us (0.84)
  local copies, waits for them, and re-layouts: 12.3 us -> 1.47 us
    unnamed x15 -> x1, local copies, waits for them, and re-layouts: 11.5 us -> 1.47 us
    reshape x1 -> x0, local copies, waits for them, and re-layouts: 0.74 us -> none  [update_states(): decay_rate.reshape(heads, 1, 1)]
where the time goes in v2:
time: 57.7 us; the launch traced here: 57.5 us
  Pallas kernels  55.4 us (96%)
  local copies, waits for them, and re-layouts  1.47 us (3%)
  between operations  0.65 us (1%)
    pallas_call x1, Pallas kernels, run_layer(): pl.pallas_call(layer_kernel, in_specs=[vmem] * 5 + [anywhere] * 4, out_sp...  46.9 us
    pallas_call x1, Pallas kernels, update_states(): pl.pallas_call(state_kernel, in_specs=[vmem] * 5 + [anywhere], out_specs=...  8.42 us
    unnamed x1, local copies, waits for them, and re-layouts  1.47 us

profile of v2, /device:TPU:0, one launch (start us, length us, event | category | flops | bytes accessed | tf_op | source)
XLA Modules:
  0.0 57.5 jit_solution(10339458426463668534)
XLA Ops:
  0.6 8.4 %states.1 = (bf16[64,4,128,128]{3,2,1,0:T(8,128)(2,1)}, bf16[64,512]{1,0:T(8,128)(2,1)}) custom-call(bf16[64,512]{1,0:T(8,128)(2,1)} %q_ref.1, bf16[64,512]{1,0:T(8,128)(2,1)} %k_ref.1, bf16[64,512]{1,0:T(8,128)(2,1)} %v_ref.1, bf16[64,512]{1,0:T(8,128)(2,1)} %g_ref.1, f32[1,4]{1,0:T(1,128)} %bitcast.7, bf16[64,4,128,128]{3,2,1,0:T(8,128)(2,1)} %s_hbm.1), custom_call_target="tpu_custom_call" | custom-call | tf_op jit(solution)/shard_map/states/pallas_call | solution.py:165
  9.1 46.9 %layer.1 = bf16[16,2048]{1,0:T(8,128)(2,1)} custom-call(bf16[64,512]{1,0:T(8,128)(2,1)} %get-tuple-element.4.head_ref, bf16[16,2048]{1,0:T(8,128)(2,1)} %hidden_ref.1, f32[1,2048]{1,0:T(1,128)} %bitcast.4, s32[2,16]{1,0:T(2,128)} %bitcast.5, f32[2,16]{1,0:T(2,128)} %bitcast.6, bf16[512,2048]{1,0:T(8,128)(2,1)} %proj_hbm.1, bf16[1,2048,2304]{2,1,0:T(8,128)(2,1)} %gate_hbm.1, ...), custom_call_target="tpu_custom_call" | custom-call | tf_op jit(solution)/shard_map/layer/pallas_call | solution.py:421
  56.0 1.5 %copy.17 = bf16[16,2048]{1,0:T(8,128)(2,1)} copy(bf16[16,2048]{1,0:T(8,128)(2,1)} %layer.1) | data formatting | bytes 131072

commit v3 on v2

--- a/solution.py
+++ b/solution.py
@@ -214,8 +214,7 @@
         for p in range(parts):
             span = pl.ds(p * depth, depth)
             loads.append(pltpu.make_async_copy(src.at[span], dst.at[span], load_sem.at[len(loads)]))
-    for load in loads:
-        load.start()
+    loads[0].start()
 
     barrier = pltpu.get_barrier_semaphore()
     pl.semaphore_signal(barrier, inc=1, device_id={"sub": sibling}, device_id_type=MESH)
@@ -317,8 +316,12 @@
         reduce_start(0, c, jnp.dot(heads[...], proj[:, columns(c, width)], preferred_element_type=jnp.float32))
 
     each(PIECES, project)
+    for load in loads[1:5]:
+        load.start()
     gather_forward(coeffs, coeff_z_sem, coeff_x_sem)
     each(PIECES, lambda c: reduce_forward(0, c))
+    for load in loads[5:9]:
+        load.start()
 
     def settle(c):
         lanes = columns(c, width)
@@ -329,6 +332,8 @@
 
     each(PIECES, settle)
     each(PIECES, lambda c: gather_forward(rows.at[c], rows_z_sem.at[c], rows_x_sem.at[c]))
+    for load in loads[9:]:
+        load.start()
     square_own[...] = jnp.zeros_like(square_own)
 
     def scale(c):

time: 57.7 us -> 57.7 us (level)
  no operation moved by 1% of the time
where the time goes in v3:
time: 57.7 us; the launch traced here: 57.5 us
  Pallas kernels  55.3 us (96%)
  local copies, waits for them, and re-layouts  1.47 us (3%)
  between operations  0.65 us (1%)
    pallas_call x1, Pallas kernels, run_layer(): pl.pallas_call(layer_kernel, in_specs=[vmem] * 5 + [anywhere] * 4, out_sp...  46.9 us
    pallas_call x1, Pallas kernels, update_states(): pl.pallas_call(state_kernel, in_specs=[vmem] * 5 + [anywhere], out_specs=...  8.42 us
    unnamed x1, local copies, waits for them, and re-layouts  1.47 us

profile of v3, /device:TPU:0, one launch (start us, length us, event | category | flops | bytes accessed | tf_op | source)
XLA Modules:
  0.0 57.5 jit_solution(13772373096901819221)
XLA Ops:
  0.6 8.4 %states.1 = (bf16[64,4,128,128]{3,2,1,0:T(8,128)(2,1)}, bf16[64,512]{1,0:T(8,128)(2,1)}) custom-call(bf16[64,512]{1,0:T(8,128)(2,1)} %q_ref.1, bf16[64,512]{1,0:T(8,128)(2,1)} %k_ref.1, bf16[64,512]{1,0:T(8,128)(2,1)} %v_ref.1, bf16[64,512]{1,0:T(8,128)(2,1)} %g_ref.1, f32[1,4]{1,0:T(1,128)} %bitcast.7, bf16[64,4,128,128]{3,2,1,0:T(8,128)(2,1)} %s_hbm.1), custom_call_target="tpu_custom_call" | custom-call | tf_op jit(solution)/shard_map/states/pallas_call | solution.py:165
  9.1 46.9 %layer.1 = bf16[16,2048]{1,0:T(8,128)(2,1)} custom-call(bf16[64,512]{1,0:T(8,128)(2,1)} %get-tuple-element.4.head_ref, bf16[16,2048]{1,0:T(8,128)(2,1)} %hidden_ref.1, f32[1,2048]{1,0:T(1,128)} %bitcast.4, s32[2,16]{1,0:T(2,128)} %bitcast.5, f32[2,16]{1,0:T(2,128)} %bitcast.6, bf16[512,2048]{1,0:T(8,128)(2,1)} %proj_hbm.1, bf16[1,2048,2304]{2,1,0:T(8,128)(2,1)} %gate_hbm.1, ...), custom_call_target="tpu_custom_call" | custom-call | tf_op jit(solution)/shard_map/layer/pallas_call | solution.py:426
  56.0 1.5 %copy.17 = bf16[16,2048]{1,0:T(8,128)(2,1)} copy(bf16[16,2048]{1,0:T(8,128)(2,1)} %layer.1) | data formatting | bytes 131072
